TPU v7x, 32 devices: a whole 2x2x4 slice. The times are simulated.
32 devices in a mesh: grp: 2 (over x), len: 16 (over z, y, core).
Axes of the slice: x: 2, y: 2, z: 4, core: 2. Of those that a mesh axis runs over, the one named last changes fastest.
Arguments:
- tin_temp: float32 [64, 512, 1024], P(None, ('grp', 'len')), parts along dimension 1, may hold values from -6 to 6
- flow_code: int32 [64, 512, 1024], P(None, ('grp', 'len')), parts along dimension 1, may hold values from 0 to 3
- speeds: float32 [2, 64], replicated, may hold values from 0.02 to 0.12
- floor_temp: float32 [32, 48, 64, 256], P(('grp', 'len')), parts along dimension 0, may hold values from -6 to 6
- material: int32 [32, 48, 64, 256], P(('grp', 'len')), parts along dimension 0, may hold values from 0 to 2
- conductivity: float32 [3], replicated, may hold values from 0.03 to 0.15
Outputs:
- tin_out: float32 [64, 512, 1024], P(None, ('grp', 'len')), parts along dimension 1
- floor_out: float32 [32, 48, 64, 256], P(('grp', 'len')), parts along dimension 0
There are 2 independent parts, one for each index of `grp`. A program takes and returns all parts, laid end to end along the dimension named above; an argument that names none is the same for every part. Nothing has to cross between parts.
Inputs may be any that keep to these rules, and one draw needn't show every extreme that they name: flow_code % 2 is 0 where the tin cell takes its length upwind value from the lower length index and 1 from the higher; flow_code // 2 likewise across the width. material ids index conductivity.
All inputs are finite; a program needn't handle non-finite values.
Results may differ from a plain program's by a relative error of at most 0.0003.
Values sent between devices are 32-bit elements; how exact they have to be, the bound alone decides.
A program may use at most 128 MiB of HBM per device.

v0:
```python
import functools

import jax
import jax.numpy as jnp
from jax import lax
from jax.experimental import pallas as pl
from jax.experimental.pallas import tpu as pltpu
from jax.sharding import PartitionSpec as P

KT = 0.1
HT = 0.2
HR = 0.2
L = 128
NQ = 4
TU = 4
FU = 3
S = 8


def kernel(n, ty, tin_h, flow_h, speeds_h, floor_h, mat_h, cond_h,
           tin_o, floor_o,
           speeds, cond, tin0, flow, tin1, floor0, mat, floor1, kh, kx, ky, kz,
           tlo, thi, tlo_s, thi_s,
           rlo, rhi, rlo_s, rhi_s,
           clo, chi, clo_s, chi_s,
           pp, bb, load_sem, send_sem, recv_sem):
    Z, R, NYW = tin_h.shape
    ZF, CX, CY = floor_h.shape
    me = lax.axis_index("len")
    c = lax.rem(me, ty)
    base = me - c
    up_ok, dn_ok = me < n - 1, me > 0
    rup_ok, rdn_ok = me + ty < n, me >= ty
    cup_ok, cdn_ok = c < ty - 1, c > 0

    loads = [pltpu.make_async_copy(a, b, load_sem.at[i]) for i, (a, b) in enumerate(
        [(tin_h, tin0), (mat_h, mat), (floor_h, floor0), (flow_h, flow)])]
    scalars = [pltpu.make_async_copy(cond_h, cond, load_sem.at[8]),
               pltpu.make_async_copy(speeds_h, speeds, load_sem.at[9])]
    for ld in scalars:
        ld.start()
    for ld in loads:
        ld.start()

    barrier = pltpu.get_barrier_semaphore()

    def hello(target):
        pl.semaphore_signal(barrier, inc=1, device_id={"len": target},
                            device_id_type=pl.DeviceIdType.MESH)

    for d in range(1, ty):
        hello(base + lax.rem(c + d, ty))
    pairs = [(rup_ok, me + ty), (rdn_ok, me - ty),
             (jnp.logical_and(c == ty - 1, up_ok), me + 1),
             (jnp.logical_and(c == 0, dn_ok), me - 1)]
    for ok, target in pairs:
        @pl.when(ok)
        def _():
            hello(target)

    row = lax.broadcasted_iota(jnp.int32, (S, L), 0)
    lane = lax.broadcasted_iota(jnp.int32, (S, L), 1)
    row_first, row_last = row == 0, row == S - 1
    lane_first, lane_last = lane == 0, lane == L - 1

    own_p = pltpu.make_async_copy(
        floor_h.at[0, pl.ds(pl.multiple_of(c * R, R), R), :],
        pp.at[0, :, pl.ds(pl.multiple_of(c * CY, CY), CY)], load_sem.at[4])
    own_b = pltpu.make_async_copy(
        tin_h.at[0, :, pl.ds(pl.multiple_of(c * CY, CY), CY)],
        bb.at[0, pl.ds(pl.multiple_of(c * R, R), R), :], load_sem.at[5])
    own_p.start()
    own_b.start()

    def remote(e, slot, src, dst, target):
        return pltpu.make_async_remote_copy(
            src_ref=src, dst_ref=dst, send_sem=send_sem.at[e, slot],
            recv_sem=recv_sem.at[e, slot], device_id={"len": target},
            device_id_type=pl.DeviceIdType.MESH)

    ZQ = Z // NQ

    def tin_msgs(e, q):
        part = pl.ds(q * ZQ, ZQ)
        return [(up_ok, dn_ok, remote(e, 12 + q, thi_s.at[e, part], tlo.at[e, part], me + 1), tlo),
                (dn_ok, up_ok, remote(e, 12 + NQ + q, tlo_s.at[e, part], thi.at[e, part], me - 1), thi)]

    def floor_msgs(e):
        if e == 0:
            return [
                (rup_ok, rdn_ok, remote(0, 2, rhi_s.at[0:2], rlo.at[0:2], me + ty), rlo),
                (rdn_ok, rup_ok, remote(0, 3, rlo_s.at[0:2], rhi.at[0:2], me - ty), rhi),
                (cup_ok, cdn_ok, remote(0, 4, chi_s.at[0:2], clo.at[0:2], me + 1), clo),
                (cdn_ok, cup_ok, remote(0, 5, clo_s.at[0:2], chi.at[0:2], me - 1), chi)]
        return [
            (rup_ok, rdn_ok, remote(1, 2, rhi_s.at[2], rlo.at[2], me + ty), rlo),
            (rdn_ok, rup_ok, remote(1, 3, rlo_s.at[2], rhi.at[2], me - ty), rhi),
            (cup_ok, cdn_ok, remote(1, 4, chi_s.at[2], clo.at[2], me + 1), clo),
            (cdn_ok, cup_ok, remote(1, 5, clo_s.at[2], chi.at[2], me - 1), chi)]

    def p_msgs(e, field):
        out = []
        for d in range(1, ty):
            t = lax.rem(c + d, ty)
            out.append(remote(
                e, 5 + d, field.at[0, pl.ds(pl.multiple_of(t * R, R), R), :],
                pp.at[e, :, pl.ds(pl.multiple_of(c * CY, CY), CY)], base + t))
        return out

    def b_msgs(e, field):
        out = []
        for d in range(1, ty):
            t = lax.rem(c + d, ty)
            out.append(remote(
                e, 8 + d, field.at[0, :, pl.ds(pl.multiple_of(t * CY, CY), CY)],
                bb.at[e, pl.ds(pl.multiple_of(c * R, R), R), :], base + t))
        return out

    def start_if(msgs):
        for ok, _, m, _ in msgs:
            @pl.when(ok)
            def _():
                m.start()

    def wait_recv_if(msgs):
        for _, ok, m, _ in msgs:
            @pl.when(ok)
            def _():
                m.wait_recv()

    def wait_send_if(msgs):
        for ok, _, m, _ in msgs:
            @pl.when(ok)
            def _():
                m.wait_send()

    def tile(ref, z, i, j):
        return ref[z, pl.ds(i * S, S), pl.ds(j * L, L)]

    for _, ok, _, buf in tin_msgs(0, 0) + floor_msgs(0):
        @pl.when(jnp.logical_not(ok))
        def _():
            buf[...] = jnp.zeros_like(buf)

    loads[0].wait()

    def pack_tin(z, carry):
        tlo_s[0, pl.ds(z, 1), :] = tin0[z, 0:1, :]
        thi_s[0, pl.ds(z, 1), :] = tin0[z, R - 1:R, :]
        return carry

    lax.fori_loop(0, Z, pack_tin, 0, unroll=8)

    peers = ty - 1
    for ok, _ in pairs:
        peers = peers + ok.astype(jnp.int32)
    pl.semaphore_wait(barrier, peers)

    t0, f0 = [tin_msgs(0, q) for q in range(NQ)], floor_msgs(0)
    t1 = [tin_msgs(1, q) for q in range(NQ)]
    p0, b0 = p_msgs(0, floor_h), b_msgs(0, tin_h)
    for m in p0 + b0:
        m.start()
    for q in range(NQ):
        start_if(t0[q])

    loads[1].wait()
    scalars[0].wait()
    c0, c1, c2 = cond[0] * 0.5, cond[1] * 0.5, cond[2] * 0.5
    NI, NJ = CX // S, CY // L

    def pack_cols(z, edge_lo, edge_hi, acc):
        lo_acc, hi_acc = acc
        here = lane == z
        lo_n = tuple(jnp.where(here, pltpu.roll(edge_lo[i], z, 1), lo_acc[i]) for i in range(NI))
        hi_n = tuple(jnp.where(here, pltpu.roll(edge_hi[i], z + 1, 1), hi_acc[i]) for i in range(NI))
        return lo_n, hi_n

    def zeros():
        zero = jnp.zeros((S, L), jnp.float32)
        return tuple(zero for _ in range(NI)), tuple(zero for _ in range(NI))

    def store_cols(slot, acc):
        for i in range(NI):
            clo_s[slot, pl.ds(i * S, S), :] = acc[0][i]
            chi_s[slot, pl.ds(i * S, S), :] = acc[1][i]

    def k_layer(z, acc):
        t = {}
        for i in range(NI):
            for j in range(NJ):
                m = tile(mat, z, i, j)
                v = jnp.where(m == 0, c0, jnp.where(m == 1, c1, c2))
                kh[z, pl.ds(i * S, S), pl.ds(j * L, L)] = v
                t[i, j] = v
        rlo_s[1, pl.ds(z, 1), :] = jnp.concatenate([t[0, j][0:1] for j in range(NJ)], 1)
        rhi_s[1, pl.ds(z, 1), :] = jnp.concatenate([t[NI - 1, j][S - 1:S] for j in range(NJ)], 1)
        return pack_cols(z, [t[i, 0] for i in range(NI)], [t[i, NJ - 1] for i in range(NI)], acc)

    store_cols(1, lax.fori_loop(0, ZF, k_layer, zeros(), unroll=8))
    loads[2].wait()

    def g_layer(z, acc):
        rlo_s[0, pl.ds(z, 1), :] = floor0[z, 0:1, :]
        rhi_s[0, pl.ds(z, 1), :] = floor0[z, CX - 1:CX, :]
        return pack_cols(z, [tile(floor0, z, i, 0) for i in range(NI)],
                         [tile(floor0, z, i, NJ - 1) for i in range(NI)], acc)

    store_cols(0, lax.fori_loop(0, ZF, g_layer, zeros(), unroll=8))
    start_if(f0)

    def floor_layer(first, src, dst, z, top, bottom):
        def put(ref, i, j, v):
            ref[z, pl.ds(i * S, S), pl.ds(j * L, L)] = v
            return v

        def next_x(roll, i, j):
            if i == NI - 1:
                return roll(i, j)
            return jnp.where(row_last, roll(i + 1, j), roll(i, j))

        def next_y(roll, i, j):
            if j == NJ - 1:
                return roll(i, j)
            return jnp.where(lane_last, roll(i, j + 1), roll(i, j))

        def rolled(get, amount, dim):
            return functools.cache(lambda i, j: pltpu.roll(get(i, j), amount, dim))

        g = functools.cache(lambda i, j: tile(src, z, i, j))
        gx, gy = rolled(g, S - 1, 0), rolled(g, L - 1, 1)
        if first:
            k = functools.cache(lambda i, j: tile(kh, z, i, j))
            k_x, k_y = rolled(k, S - 1, 0), rolled(k, L - 1, 1)

            def face_x(i, j):
                v = k(i, j) + next_x(k_x, i, j)
                return put(kx, i, j, jnp.where(row_last, 0.0, v) if i == NI - 1 else v)

            def face_y(i, j):
                v = k(i, j) + next_y(k_y, i, j)
                return put(ky, i, j, jnp.where(lane_last, 0.0, v) if j == NJ - 1 else v)

            def face_z(i, j):
                return put(kz, i, j, k(i, j) if bottom else k(i, j) + tile(kh, z + 1, i, j))
        else:
            def face_x(i, j):
                return tile(kx, z, i, j)

            def face_y(i, j):
                return tile(ky, z, i, j)

            def face_z(i, j):
                return tile(kz, z, i, j)

        fx = functools.cache(lambda i, j: face_x(i, j) * (next_x(gx, i, j) - g(i, j)))
        fy = functools.cache(lambda i, j: face_y(i, j) * (next_y(gy, i, j) - g(i, j)))
        sx, sy = rolled(fx, 1, 0), rolled(fy, 1, 1)
        for i in range(NI):
            for j in range(NJ):
                px = jnp.where(row_first, sx(i - 1, j) if i else 0.0, sx(i, j))
                py = jnp.where(lane_first, sy(i, j - 1) if j else 0.0, sy(i, j))
                v = g(i, j)
                if bottom:
                    new = v - face_z(i, j) * v
                else:
                    new = v + face_z(i, j) * (tile(src, z + 1, i, j) - v)
                if not top:
                    new = new - tile(kz, z - 1, i, j) * (v - tile(src, z - 1, i, j))
                put(dst, i, j, new + ((fx(i, j) - px) + (fy(i, j) - py)))

    def floor_sweep(first, src, dst):
        floor_layer(first, src, dst, 0, True, False)

        def body(z, carry):
            floor_layer(first, src, dst, z, False, False)
            return carry

        lax.fori_loop(1, ZF - 1, body, 0, unroll=FU)
        floor_layer(first, src, dst, ZF - 1, False, True)

    def floor_edges(e, src, dst):
        g = 2 * e
        slot = 0 if e == 0 else 2
        rlo[slot] = (rlo_s[1] + rlo[1]) * (rlo[slot] - rlo_s[slot])
        rhi[slot] = (rhi_s[1] + rhi[1]) * (rhi[slot] - rhi_s[slot])
        clo[slot] = (clo_s[1] + clo[1]) * (clo[slot] - clo_s[slot])
        chi[slot] = (chi_s[1] + chi[1]) * (chi[slot] - chi_s[slot])
        dst[0] = dst[0] + HR * (bb[e] - src[0])

        def body(z, acc):
            row_lo, row_hi = rlo[slot, pl.ds(z, 1), :], rhi[slot, pl.ds(z, 1), :]
            t = {(i, j): tile(dst, z, i, j) for i in range(NI) for j in range(NJ)}
            for j in range(NJ):
                t[0, j] = t[0, j] + jnp.where(row_first, row_lo[:, j * L:j * L + L], 0.0)
                t[NI - 1, j] = t[NI - 1, j] + jnp.where(
                    row_last, row_hi[:, j * L:j * L + L], 0.0)
            for i in range(NI):
                low = pltpu.roll(clo[slot, pl.ds(i * S, S), :], lax.rem(L - z, L), 1)
                high = pltpu.roll(chi[slot, pl.ds(i * S, S), :], L - 1 - z, 1)
                t[i, 0] = t[i, 0] + jnp.where(lane_first, low, 0.0)
                t[i, NJ - 1] = t[i, NJ - 1] + jnp.where(lane_last, high, 0.0)
            for (i, j), v in t.items():
                dst[z, pl.ds(i * S, S), pl.ds(j * L, L)] = v
            if e == 1:
                return acc
            rlo_s[2, pl.ds(z, 1), :] = jnp.concatenate([t[0, j][0:1] for j in range(NJ)], 1)
            rhi_s[2, pl.ds(z, 1), :] = jnp.concatenate([t[NI - 1, j][S - 1:S] for j in range(NJ)], 1)
            return pack_cols(z, [t[i, 0] for i in range(NI)],
                             [t[i, NJ - 1] for i in range(NI)], acc)

        if e == 0:
            store_cols(2, lax.fori_loop(0, ZF, body, zeros(), unroll=8))
        else:
            lax.fori_loop(0, ZF, body, 0, unroll=8)

    NH, NK = R // S, NYW // L

    def tin_layer(e, src, dst, z, zu, zd, top):
        s_x, s_y = speeds[0, z], speeds[1, z]
        keep = (1.0 - 6.0 * KT) - s_x - s_y
        first_row, last_row = [], []
        before, after = tlo[e, pl.ds(z, 1), :], thi[e, pl.ds(z, 1), :]
        u = functools.cache(lambda h, k: tile(src, z, h, k))
        rd = functools.cache(lambda h, k: pltpu.roll(u(h, k), 1, 0))
        ru = functools.cache(lambda h, k: pltpu.roll(u(h, k), S - 1, 0))
        ld = functools.cache(lambda h, k: pltpu.roll(u(h, k), 1, 1))
        lu = functools.cache(lambda h, k: pltpu.roll(u(h, k), L - 1, 1))
        span = [(h, k) for k in range(NK) for h in range(NH)]
        for h, k in span:
            v = u(h, k)
            below = before[:, k * L:k * L + L] if h == 0 else rd(h - 1, k)
            above = after[:, k * L:k * L + L] if h == NH - 1 else ru(h + 1, k)
            xm = jnp.where(row_first, below, rd(h, k))
            xp = jnp.where(row_last, above, ru(h, k))
            ym = jnp.where(lane_first, 0.0 if k == 0 else ld(h, k - 1), ld(h, k))
            yp = jnp.where(lane_last, 0.0 if k == NK - 1 else lu(h, k + 1), lu(h, k))
            f = tile(flow, z, h, k)
            total = ((xm + xp) + (ym + yp)) + (tile(src, zu, h, k) + tile(src, zd, h, k))
            new = keep * v + KT * total
            new = new + s_x * jnp.where((f & 1) == 0, xm, xp)
            new = new + s_y * jnp.where(f < 2, ym, yp)
            if top:
                new = new + HT * (pp[e, pl.ds(h * S, S), pl.ds(k * L, L)] - v)
            dst[z, pl.ds(h * S, S), pl.ds(k * L, L)] = new
            if h == 0:
                first_row.append(new[0:1])
            if h == NH - 1:
                last_row.append(new[S - 1:S])
        if e == 0:
            tlo_s[1, pl.ds(z, 1), :] = jnp.concatenate(first_row, 1)
            thi_s[1, pl.ds(z, 1), :] = jnp.concatenate(last_row, 1)

    def tin_sweep(e, src, dst, q):
        if q == 0:
            tin_layer(e, src, dst, 0, 1, 0, True)

        def body(z, carry):
            tin_layer(e, src, dst, z, jnp.minimum(z + 1, Z - 1), z - 1, False)
            return carry

        lax.fori_loop(max(1, q * ZQ), (q + 1) * ZQ, body, 0, unroll=TU)

    floor_sweep(True, floor0, floor1)

    loads[3].wait()
    scalars[1].wait()
    for m in p0:
        m.wait_recv()
    own_p.wait()
    b1 = b_msgs(1, tin1)
    own_b1 = pltpu.make_async_copy(
        tin1.at[0, :, pl.ds(pl.multiple_of(c * CY, CY), CY)],
        bb.at[1, pl.ds(pl.multiple_of(c * R, R), R), :], load_sem.at[7])
    for q in range(NQ):
        wait_recv_if(t0[q])
        tin_sweep(0, tin0, tin1, q)
        start_if(t1[q])
        if q == 0:
            for m in b1:
                m.start()
            own_b1.start()

    wait_recv_if(f0)
    for m in b0:
        m.wait_recv()
    own_b.wait()
    wait_send_if(f0)
    floor_edges(0, floor0, floor1)
    f1, p1 = floor_msgs(1), p_msgs(1, floor1)
    for m in p1:
        m.start()
    start_if(f1)
    own_p1 = pltpu.make_async_copy(
        floor1.at[0, pl.ds(pl.multiple_of(c * R, R), R), :],
        pp.at[1, :, pl.ds(pl.multiple_of(c * CY, CY), CY)], load_sem.at[6])
    own_p1.start()

    floor_sweep(False, floor1, floor_o)
    for m in p1:
        m.wait_recv()
    own_p1.wait()
    for q in range(NQ):
        wait_recv_if(t1[q])
        tin_sweep(1, tin1, tin_o, q)

    wait_recv_if(f1)
    for m in b1:
        m.wait_recv()
    own_b1.wait()
    wait_send_if(f1)
    floor_edges(1, floor1, floor_o)

    for q in range(NQ):
        wait_send_if(t0[q])
        wait_send_if(t1[q])
    for m in p0 + b0 + p1 + b1:
        m.wait_send()


def local(n, ty, tin_temp, flow_code, speeds, floor_temp, material, conductivity):
    tin_shape = tin_temp.shape
    floor_shape = floor_temp.shape[1:]
    Z, R, NYW = tin_shape
    ZF, CX, CY = floor_shape
    f32, i32 = jnp.float32, jnp.int32
    V = pltpu.VMEM
    tin_v, floor_v = V(tin_shape, f32), V(floor_shape, f32)
    edge_t = V((2, Z, NYW), f32)
    edge_r = V((3, ZF, CY), f32)
    edge_c = V((3, CX, L), f32)
    tin_out, floor_out = pl.pallas_call(
        functools.partial(kernel, n, ty),
        out_shape=OUT(tin_shape, floor_shape),
        in_specs=[pl.BlockSpec(memory_space=m) for m in
                  (pltpu.HBM,) * 6],
        out_specs=[pl.BlockSpec(memory_space=pltpu.VMEM)] * 2,
        scratch_shapes=[
            pltpu.SMEM(speeds.shape, f32), pltpu.SMEM(conductivity.shape, f32),
            tin_v, V(tin_shape, i32), tin_v, floor_v, V(floor_shape, i32), floor_v,
            floor_v, floor_v, floor_v, floor_v,
            edge_t, edge_t, edge_t, edge_t,
            edge_r, edge_r, edge_r, edge_r,
            edge_c, edge_c, edge_c, edge_c,
            V((2, R, NYW), f32), V((2, CX, CY), f32),
            pltpu.SemaphoreType.DMA((10,)),
            pltpu.SemaphoreType.DMA((2, 12 + 2 * NQ)),
            pltpu.SemaphoreType.DMA((2, 12 + 2 * NQ)),
        ],
        compiler_params=pltpu.CompilerParams(
            collective_id=0, has_side_effects=True, vmem_limit_bytes=44 * 1024 * 1024),
        cost_estimate=pl.CostEstimate(flops=120_000_000, bytes_accessed=23_000_000, transcendentals=0),
    )(tin_temp, flow_code, pltpu.with_memory_space_constraint(speeds, pltpu.HBM), floor_temp[0],
      material[0], pltpu.with_memory_space_constraint(conductivity, pltpu.HBM))
    return tin_out, floor_out[None]


def OUT(tin_shape, floor_shape):
    return [pltpu.VMEM(tin_shape, jnp.float32), pltpu.VMEM(floor_shape, jnp.float32)]


def solution(mesh):
    n = mesh.shape["len"]
    split = ("grp", "len")
    placed = (P(None, split, None), P(None, split, None), P(),
              P(split, None, None, None), P(split, None, None, None), P())

    def whole(tin_temp, flow_code, speeds, floor_temp, material, conductivity):
        ty = tin_temp.shape[2] // floor_temp.shape[3]
        return jax.shard_map(
            functools.partial(local, n, ty),
            mesh=mesh,
            in_specs=placed,
            out_specs=(P(None, split, None), P(split, None, None, None)),
            check_vma=False,
        )(tin_temp, flow_code, speeds, floor_temp, material, conductivity)

    return whole
```

profile of v0, /device:TPU:1, one launch (start us, length us, event | category | flops | bytes accessed | tf_op | source)
XLA Modules:
  0.0 34.0 jit_solution(14640654202704423465)
XLA Ops:
  0.6 29.7 %shard_map.77 = (f32[64,16,1024]{2,1,0:T(8,128)S(1)}, f32[48,64,256]{2,1,0:T(8,128)S(1)}) custom-call(f32[64,16,1024]{2,1,0:T(8,128)} %tin_h.1, s32[64,16,1024]{2,1,0:T(8,128)} %flow_h.1, f32[2,64]{1,0:T(2,128)} %speeds_h.1, f32[48,64,256]{2,1,0:T(8,128)} %bitcast.4, s32[48,64,256]{2,1,0:T(8,128)} %bitcast.5, f32[3]{0:T(128)} %cond_h.1), custom_call_target="tpu_custom_call" | custom-call | flops 120000000 | bytes 23000000 | tf_op jit(solution)/shard_map/pallas_call | solution.py:432
  30.3 2.0 %copy.10 = f32[64,16,1024]{2,1,0:T(8,128)} copy(f32[64,16,1024]{2,1,0:T(8,128)S(1)} %get-tuple-element.6) | data formatting | bytes 8388608
  32.3 1.7 %copy.11 = f32[1,48,64,256]{3,2,1,0:T(8,128)} copy(f32[1,48,64,256]{3,2,1,0:T(8,128)S(1)} %bitcast.3) | data formatting | bytes 6291456
where the time goes:
time: 34.3 us; the launch traced here: 34 us
  Pallas kernels  29.7 us (87%)
  local copies, waits for them, and re-layouts  3.68 us (11%)
  between operations  0.64 us (2%)
    pallas_call x1, Pallas kernels, local(): pl.pallas_call(functools.partial(kernel, n, ty), out_shape=OUT(tin_shape,...  29.7 us
    unnamed x2, local copies, waits for them, and re-layouts  3.68 us

commit v1 on v0

v1 whole, which is shorter than its diff:
```python
import functools

import jax
import jax.numpy as jnp
from jax import lax
from jax.experimental import pallas as pl
from jax.experimental.pallas import tpu as pltpu
from jax.sharding import PartitionSpec as P

KT = 0.1
HT = 0.2
HR = 0.2
L = 128
S = 8
NQ = 4
FQ = 2
TU = 2
FU = 1
PU = 2


def kernel(n, ty, tin_h, flow_h, speeds_h, floor_h, mat_h, cond_h,
           tin_o, floor_o,
           speeds, cond, tin0, flow, tin1, floor0, mat, floor1, kh, kx, ky, kz, pz,
           cs, cl, cr, kd, fd, pp, bb, load_sem, send_sem, recv_sem):
    Z, R, NYW = tin_h.shape
    ZF, CX, CY = floor_h.shape
    NH, NK = R // S, NYW // L
    NI, NJ = CX // S, CY // L
    ZQ, ZC = Z // NQ, ZF // FQ
    me = lax.axis_index("len")
    c = lax.rem(me, ty)
    base = me - c
    up_ok, dn_ok = me < n - 1, me > 0
    rup_ok, rdn_ok = me + ty < n, me >= ty
    cup_ok, cdn_ok = c < ty - 1, c > 0

    numbers = iter(range(10 ** 6))

    def local_copy(src, dst):
        return pltpu.make_async_copy(src, dst, load_sem.at[next(numbers)])

    get_cond, get_speeds = local_copy(cond_h, cond), local_copy(speeds_h, speeds)
    get_floor = []
    for q in range(FQ):
        part = pl.ds(q * ZC, ZC)
        get_floor.append(
            [local_copy(mat_h.at[part, :, pl.ds(j * L, L)], mat.at[part, j, pl.ds(S, CX), :]) for j in range(NJ)]
            + [local_copy(floor_h.at[part, :, pl.ds(j * L, L)], floor0.at[part, j, pl.ds(S, CX), :])
               for j in range(NJ)])
    get_tin = []
    for q in range(NQ):
        part = pl.ds(q * ZQ, ZQ)
        get_tin.append(
            [local_copy(tin_h.at[part, :, pl.ds(k * L, L)], tin0.at[pl.ds(q * ZQ + 1, ZQ), k, pl.ds(S, R), :])
             for k in range(NK)] + [local_copy(flow_h.at[part], flow.at[part])])
    get_cond.start()
    get_speeds.start()

    barrier = pltpu.get_barrier_semaphore()

    def hello(target):
        pl.semaphore_signal(barrier, inc=1, device_id={"len": target},
                            device_id_type=pl.DeviceIdType.MESH)

    for d in range(1, ty):
        hello(base + lax.rem(c + d, ty))
    pairs = [(rup_ok, me + ty), (rdn_ok, me - ty),
             (jnp.logical_and(c == ty - 1, up_ok), me + 1),
             (jnp.logical_and(c == 0, dn_ok), me - 1)]
    for ok, target in pairs:
        @pl.when(ok)
        def _():
            hello(target)

    for group in get_floor + get_tin:
        for ld in group:
            ld.start()

    row = lax.broadcasted_iota(jnp.int32, (S, L), 0)
    lane = lax.broadcasted_iota(jnp.int32, (S, L), 1)
    row_first = row == 0
    lane_first, lane_last = lane == 0, lane == L - 1
    lane_even = (lane & 1) == 0
    zero = jnp.zeros((S, L), jnp.float32)

    links = iter(range(10 ** 6))

    def remote(src, dst, target):
        e = next(links)
        return pltpu.make_async_remote_copy(
            src_ref=src, dst_ref=dst, send_sem=send_sem.at[e],
            recv_sem=recv_sem.at[e], device_id={"len": target},
            device_id_type=pl.DeviceIdType.MESH)

    def both_ways(up, down, ok_up, ok_dn):
        return [(ok_up, ok_dn, up), (ok_dn, ok_up, down)]

    lo, hi = S - 1, S + R
    flo, fhi = S - 1, S + CX
    planes = pl.ds(1, Z)
    t0 = both_ways(
        [remote(tin_h.at[:, R - 1, pl.ds(k * L, L)], tin0.at[planes, k, lo, :], me + 1) for k in range(NK)],
        [remote(tin_h.at[:, 0, pl.ds(k * L, L)], tin0.at[planes, k, hi, :], me - 1) for k in range(NK)],
        up_ok, dn_ok)
    layers = pl.ds(0, ZF)
    r0 = both_ways(
        [remote(a.at[:, CX - 1, pl.ds(j * L, L)], b.at[layers, j, flo, :], me + ty)
         for a, b in ((floor_h, floor0), (mat_h, mat)) for j in range(NJ)],
        [remote(a.at[:, 0, pl.ds(j * L, L)], b.at[layers, j, fhi, :], me - ty)
         for a, b in ((floor_h, floor0), (mat_h, mat)) for j in range(NJ)],
        rup_ok, rdn_ok)
    c0 = both_ways([remote(cs.at[0:2], cl.at[0:2], me + 1)], [remote(cs.at[0:2], cr.at[0:2], me - 1)],
                   cup_ok, cdn_ok)
    t1 = both_ways([remote(tin1.at[planes, :, S + R - 1, :], tin1.at[planes, :, lo, :], me + 1)],
                   [remote(tin1.at[planes, :, S, :], tin1.at[planes, :, hi, :], me - 1)],
                   up_ok, dn_ok)
    r1 = both_ways([remote(floor1.at[layers, :, S + CX - 1, :], floor1.at[layers, :, flo, :], me + ty)],
                   [remote(floor1.at[layers, :, S, :], floor1.at[layers, :, fhi, :], me - ty)],
                   rup_ok, rdn_ok)
    c1 = both_ways([remote(cs.at[2], cl.at[2], me + 1)], [remote(cs.at[2], cr.at[2], me - 1)],
                   cup_ok, cdn_ok)

    def floor_part(field, t):
        return field.at[0, :, pl.ds(pl.multiple_of(S + t * R, S), R), :]

    def tin_part(field, t):
        return field.at[1, pl.ds(NJ * t, NJ), pl.ds(S, R), :]

    def p_into(e):
        return pp.at[e, pl.ds(NJ * c, NJ), :, :]

    def b_into(e):
        return bb.at[e, :, pl.ds(pl.multiple_of(c * R, S), R), :]

    def to_group(part, into):
        out = []
        for d in range(1, ty):
            t = lax.rem(c + d, ty)
            out.append(remote(part(t), into, base + t))
        return out

    p0 = to_group(functools.partial(floor_part, floor0), p_into(0))
    b0 = to_group(functools.partial(tin_part, tin0), b_into(0))
    p1 = to_group(functools.partial(floor_part, floor1), p_into(1))
    b1 = to_group(functools.partial(tin_part, tin1), b_into(1))
    own_p0, own_p1 = local_copy(floor_part(floor0, c), p_into(0)), local_copy(floor_part(floor1, c), p_into(1))
    own_b0, own_b1 = local_copy(tin_part(tin0, c), b_into(0)), local_copy(tin_part(tin1, c), b_into(1))

    def start_if(msgs):
        for ok, _, copies in msgs:
            @pl.when(ok)
            def _():
                for m in copies:
                    m.start()

    def wait_recv_if(msgs):
        for _, ok, copies in msgs:
            @pl.when(ok)
            def _():
                for m in copies:
                    m.wait_recv()

    def wait_send_if(msgs):
        for ok, _, copies in msgs:
            @pl.when(ok)
            def _():
                for m in copies:
                    m.wait_send()

    def clear(ok, fields, first):
        @pl.when(jnp.logical_not(ok))
        def _():
            for ref in fields:
                def body(z, carry):
                    for k in range(ref.shape[1]):
                        ref[z, k, pl.ds(first, S), :] = zero
                    return carry

                lax.fori_loop(0, ref.shape[0], body, 0)

    clear(dn_ok, (tin0, tin1), 0)
    clear(up_ok, (tin0, tin1), S + R)
    clear(rdn_ok, (floor0, floor1), 0)
    clear(rup_ok, (floor0, floor1), S + CX)
    for ok, ref in ((cdn_ok, cl), (cup_ok, cr)):
        @pl.when(jnp.logical_not(ok))
        def _():
            ref[...] = jnp.zeros_like(ref)
    cs[...] = jnp.zeros_like(cs)
    for ref in (floor0, floor1, kh):
        for j in range(NJ):
            for i in range(NI):
                ref[ZF, j, pl.ds(S + i * S, S), :] = zero

    peers = ty - 1
    for ok, _ in pairs:
        peers = peers + ok.astype(jnp.int32)
    pl.semaphore_wait(barrier, peers)
    start_if(r0)
    start_if(t0)

    get_cond.wait()
    k0, k1, k2 = cond[0] * 0.5, cond[1] * 0.5, cond[2] * 0.5

    def lookup(m):
        return jnp.where(m == 0, k0, jnp.where(m == 1, k1, k2))

    def pack_columns(slot, z, i, first, last):
        mine = lax.shift_right_logical(lane, 1) == z
        both = pltpu.roll(jnp.where(lane_last, last, first), 2 * z + 1, 1)
        pltpu.store(cs.at[slot, pl.ds(i * S, S), :], both, mask=mine)

    def prepare(z, carry):
        for i in range(NI):
            at = pl.ds(S + i * S, S)
            k = [lookup(mat[z, j, at, :]) for j in range(NJ)]
            for j in range(NJ):
                kh[z, j, at, :] = k[j]
            pack_columns(0, z, i, k[0], k[NJ - 1])
            pack_columns(1, z, i, floor0[z, 0, at, :], floor0[z, NJ - 1, at, :])
        return carry

    for q in range(FQ):
        for ld in get_floor[q]:
            ld.wait()
        lax.fori_loop(q * ZC, (q + 1) * ZC, prepare, 0, unroll=PU)
    start_if(c0)
    for m in p0:
        m.start()
    own_p0.start()

    def tin_ghosts(e, src):
        for k in range(NK):
            for h in range(NH):
                at = pl.ds(S + h * S, S)
                u = src[1, k, at, :]
                src[0, k, at, :] = u + (HT / KT) * (pp[e, k, pl.ds(h * S, S), :] - u)

    def tin_copy_last(src):
        for k in range(NK):
            src[Z + 1, k, pl.ds(S, R), :] = src[Z, k, pl.ds(S, R), :]

    def tin_layer(src, put, z):
        s_x, s_y = speeds[0, z], speeds[1, z]
        keep = (1.0 - 6.0 * KT) - s_x - s_y

        def at(p, h, k, shift=0):
            return src[p, k, pl.ds(S + h * S + shift, S), :]

        u = functools.cache(lambda h, k: at(z + 1, h, k))
        ld = functools.cache(lambda h, k: pltpu.roll(u(h, k), 1, 1))
        lu = functools.cache(lambda h, k: pltpu.roll(u(h, k), L - 1, 1))
        for k in range(NK):
            for h in range(NH):
                xm, xp = at(z + 1, h, k, -1), at(z + 1, h, k, 1)
                ym = jnp.where(lane_first, 0.0 if k == 0 else ld(h, k - 1), ld(h, k))
                yp = jnp.where(lane_last, 0.0 if k == NK - 1 else lu(h, k + 1), lu(h, k))
                f = flow[z, pl.ds(h * S, S), pl.ds(k * L, L)]
                total = ((xm + xp) + (ym + yp)) + (at(z, h, k) + at(z + 2, h, k))
                new = keep * u(h, k) + KT * total
                new = new + s_x * jnp.where((f & 1) == 0, xm, xp)
                new = new + s_y * jnp.where(f < 2, ym, yp)
                put(z, h, k, new)

    def put_tin1(z, h, k, v):
        tin1[z + 1, k, pl.ds(S + h * S, S), :] = v

    def put_tin_o(z, h, k, v):
        tin_o[z, pl.ds(h * S, S), pl.ds(k * L, L)] = v

    def tin_range(src, put, first, last):
        def body(z, carry):
            tin_layer(src, put, z)
            return carry

        lax.fori_loop(first, last, body, 0, unroll=TU)

    def edge_flux(slot):
        for i in range(NI):
            at = pl.ds(i * S, S)

            def beside(s):
                return jnp.where(lane_even, pltpu.roll(cr[s, at, :], L - 1, 1), pltpu.roll(cl[s, at, :], 1, 1))

            if slot == 1:
                k = cs[0, at, :] + beside(0)
                kd[at, :] = jnp.where(lane_even, k, -k)
            fd[at, :] = kd[at, :] * (beside(slot) - cs[slot, at, :])

    def contact_flux(e, src):
        for j in range(NJ):
            for i in range(NI):
                at = pl.ds(i * S, S)
                pz[j, at, :] = HR * (src[0, j, pl.ds(S + i * S, S), :] - bb[e, j, at, :])

    def floor_layer(first, src, put, z):
        def at(ref, p, j, i, shift=0):
            return ref[p, j, pl.ds(S + i * S + shift, S), :]

        def face_x(j, i):
            if first:
                v = at(kh, z, j, i) + at(kh, z, j, i, 1)
                kx[z, j, pl.ds(S + i * S, S), :] = v
                return v
            return at(kx, z, j, i)

        def flux_x(j, i):
            return face_x(j, i) * (at(src, z, j, i, 1) - at(src, z, j, i))

        rx = [pltpu.roll(flux_x(j, -1), 1, 0) for j in range(NJ)]
        for i in range(NI):
            own = pl.ds(i * S, S)
            g = [at(src, z, j, i) for j in range(NJ)]
            if first:
                k = [at(kh, z, j, i) for j in range(NJ)]
                kr = [pltpu.roll(v, L - 1, 1) for v in k]
                fy_k = []
                for j in range(NJ):
                    v = k[j] + (kr[j] if j == NJ - 1 else jnp.where(lane_last, kr[j + 1], kr[j]))
                    ky[z, j, own, :] = v
                    fy_k.append(v)
            else:
                fy_k = [ky[z, j, own, :] for j in range(NJ)]
            edge = pltpu.roll(fd[own, :], L - 1 - 2 * z, 1)
            gr = [pltpu.roll(v, L - 1, 1) for v in g]
            fy = []
            for j in range(NJ):
                if j == NJ - 1:
                    fy.append(jnp.where(lane_last, edge, fy_k[j] * (gr[j] - g[j])))
                else:
                    fy.append(fy_k[j] * (jnp.where(lane_last, gr[j + 1], gr[j]) - g[j]))
            fr = [pltpu.roll(v, 1, 1) for v in fy]
            new = []
            for j in range(NJ):
                py = jnp.where(lane_first, fr[j - 1] if j else edge, fr[j])
                fx = flux_x(j, i)
                rolled = pltpu.roll(fx, 1, 0)
                px = jnp.where(row_first, rx[j], rolled)
                rx[j] = rolled
                if first:
                    k_z = k[j] + at(kh, z + 1, j, i)
                    kz[z, j, own, :] = k_z
                else:
                    k_z = kz[z, j, own, :]
                fz = k_z * (at(src, z + 1, j, i) - g[j])
                v = (g[j] + (fz - pz[j, own, :])) + ((fx - px) + (fy[j] - py))
                pz[j, own, :] = fz
                put(z, j, i, v)
                new.append(v)
            if first:
                pack_columns(2, z, i, new[0], new[NJ - 1])

    def put_floor1(z, j, i, v):
        floor1[z, j, pl.ds(S + i * S, S), :] = v

    def put_floor_o(z, j, i, v):
        floor_o[z, pl.ds(i * S, S), pl.ds(j * L, L)] = v

    def floor_sweep(first, src, put):
        def body(z, carry):
            floor_layer(first, src, put, z)
            return carry

        lax.fori_loop(0, ZF, body, 0, unroll=FU)

    get_speeds.wait()
    for ld in get_tin[0]:
        ld.wait()
    for m in b0:
        m.start()
    own_b0.start()
    for m in p0:
        m.wait_recv()
    own_p0.wait()
    tin_ghosts(0, tin0)
    wait_recv_if(t0)
    for q in range(NQ):
        if q < NQ - 1:
            for ld in get_tin[q + 1]:
                ld.wait()
        else:
            tin_copy_last(tin0)
        tin_range(tin0, put_tin1, q * ZQ, (q + 1) * ZQ)
    tin_copy_last(tin1)
    start_if(t1)
    for m in b1:
        m.start()
    own_b1.start()

    wait_recv_if(r0)

    def k_halo(z, carry):
        for j in range(NJ):
            for ok, at in ((rdn_ok, pl.ds(0, S)), (rup_ok, pl.ds(S + CX, S))):
                kh[z, j, at, :] = lookup(mat[z, j, at, :]) * ok.astype(jnp.float32)
        return carry

    lax.fori_loop(0, ZF, k_halo, 0, unroll=4)
    wait_recv_if(c0)
    edge_flux(1)
    for m in b0:
        m.wait_recv()
    own_b0.wait()
    contact_flux(0, floor0)
    floor_sweep(True, floor0, put_floor1)
    start_if(r1)
    start_if(c1)
    for m in p1:
        m.start()
    own_p1.start()

    wait_recv_if(t1)
    for m in p1:
        m.wait_recv()
    own_p1.wait()
    tin_ghosts(1, tin1)
    tin_range(tin1, put_tin_o, 0, Z)

    wait_recv_if(r1)
    wait_recv_if(c1)
    for m in b1:
        m.wait_recv()
    own_b1.wait()
    edge_flux(2)
    contact_flux(1, floor1)
    floor_sweep(False, floor1, put_floor_o)

    for msgs in (t0, r0, c0, t1, r1, c1):
        wait_send_if(msgs)
    for m in p0 + b0 + p1 + b1:
        m.wait_send()


def local(n, ty, tin_temp, flow_code, speeds, floor_temp, material, conductivity):
    tin_shape = tin_temp.shape
    floor_shape = floor_temp.shape[1:]
    Z, R, NYW = tin_shape
    ZF, CX, CY = floor_shape
    NK, NJ = NYW // L, CY // L
    f32, i32 = jnp.float32, jnp.int32
    V = pltpu.VMEM
    tin_v, floor_v = V((Z + 2, NK, R + 2 * S, L), f32), V((ZF + 1, NJ, CX + 2 * S, L), f32)
    n_local = 6 + FQ * 2 * NJ + NQ * (NK + 1)
    n_remote = 2 * NK + 4 * NJ + 8 + 4 * (ty - 1)
    tin_out, floor_out = pl.pallas_call(
        functools.partial(kernel, n, ty),
        out_shape=[V(tin_shape, f32), V(floor_shape, f32)],
        in_specs=[pl.BlockSpec(memory_space=pltpu.HBM)] * 6,
        out_specs=[pl.BlockSpec(memory_space=pltpu.VMEM)] * 2,
        scratch_shapes=[
            pltpu.SMEM(speeds.shape, f32), pltpu.SMEM(conductivity.shape, f32),
            tin_v, V(tin_shape, i32), tin_v, floor_v, V((ZF, NJ, CX + 2 * S, L), i32), floor_v,
            floor_v, V((ZF, NJ, CX + S, L), f32), V((ZF, NJ, CX, L), f32), V((ZF, NJ, CX, L), f32),
            V((NJ, CX, L), f32),
            V((3, CX, L), f32), V((3, CX, L), f32), V((3, CX, L), f32), V((CX, L), f32), V((CX, L), f32),
            V((2, NK, R, L), f32), V((2, NJ, CX, L), f32),
            pltpu.SemaphoreType.DMA((n_local,)),
            pltpu.SemaphoreType.DMA((n_remote,)),
            pltpu.SemaphoreType.DMA((n_remote,)),
        ],
        compiler_params=pltpu.CompilerParams(
            collective_id=0, has_side_effects=True, vmem_limit_bytes=52 * 1024 * 1024),
        cost_estimate=pl.CostEstimate(flops=120_000_000, bytes_accessed=23_000_000, transcendentals=0),
    )(tin_temp, flow_code, pltpu.with_memory_space_constraint(speeds, pltpu.HBM), floor_temp[0],
      material[0], pltpu.with_memory_space_constraint(conductivity, pltpu.HBM))
    return tin_out, floor_out[None]


def solution(mesh):
    n = mesh.shape["len"]
    split = ("grp", "len")
    placed = (P(None, split, None), P(None, split, None), P(),
              P(split, None, None, None), P(split, None, None, None), P())

    def whole(tin_temp, flow_code, speeds, floor_temp, material, conductivity):
        ty = tin_temp.shape[2] // floor_temp.shape[3]
        return jax.shard_map(
            functools.partial(local, n, ty),
            mesh=mesh,
            in_specs=placed,
            out_specs=(P(None, split, None), P(split, None, None, None)),
            check_vma=False,
        )(tin_temp, flow_code, speeds, floor_temp, material, conductivity)

    return whole
```

time: 34.3 us -> 51.9 us (1.51)
  Pallas kernels: 29.7 us -> 47.1 us
    pallas_call x1, Pallas kernels: 29.7 us -> 47.1 us  [local(): pl.pallas_call(functools.partial(kernel, n, ty), out_shape=[V(tin_shape,...]
where the time goes in v1:
time: 51.9 us; the launch traced here: 51.4 us
  Pallas kernels  47.1 us (91%)
  local copies, waits for them, and re-layouts  3.68 us (7%)
  between operations  0.64 us (1%)
    pallas_call x1, Pallas kernels, local(): pl.pallas_call(functools.partial(kernel, n, ty), out_shape=[V(tin_shape,...  47.1 us
    unnamed x2, local copies, waits for them, and re-layouts  3.68 us

profile of v1, /device:TPU:1, one launch (start us, length us, event | category | flops | bytes accessed | tf_op | source)
XLA Modules:
  0.0 51.4 jit_solution(1932803654131704625)
XLA Ops:
  0.6 47.1 %shard_map.77 = (f32[64,16,1024]{2,1,0:T(8,128)S(1)}, f32[48,64,256]{2,1,0:T(8,128)S(1)}) custom-call(f32[64,16,1024]{2,1,0:T(8,128)} %tin_h.1, s32[64,16,1024]{2,1,0:T(8,128)} %flow_h.1, f32[2,64]{1,0:T(2,128)} %speeds_h.1, f32[48,64,256]{2,1,0:T(8,128)} %bitcast.4, s32[48,64,256]{2,1,0:T(8,128)} %bitcast.5, f32[3]{0:T(128)} %cond_h.1), custom_call_target="tpu_custom_call" | custom-call | flops 120000000 | bytes 23000000 | tf_op jit(solution)/shard_map/pallas_call | solution.py:446
  47.7 2.0 %copy.10 = f32[64,16,1024]{2,1,0:T(8,128)} copy(f32[64,16,1024]{2,1,0:T(8,128)S(1)} %get-tuple-element.6) | data formatting | bytes 8388608
  49.8 1.7 %copy.11 = f32[1,48,64,256]{3,2,1,0:T(8,128)} copy(f32[1,48,64,256]{3,2,1,0:T(8,128)S(1)} %bitcast.3) | data formatting | bytes 6291456

commit v2 on v1

--- a/solution.py
+++ b/solution.py
@@ -14,14 +14,14 @@
 S = 8
 NQ = 4
 FQ = 2
-TU = 2
-FU = 1
-PU = 2
+TU = 8
+FU = 8
+PU = 8
 
 
 def kernel(n, ty, tin_h, flow_h, speeds_h, floor_h, mat_h, cond_h,
            tin_o, floor_o,
-           speeds, cond, tin0, flow, tin1, floor0, mat, floor1, kh, kx, ky, kz, pz,
+           speeds, cond, tin0, flow, tin1, floor0, mat, floor1, kh, kx, kyp, kym, kz, pz,
            cs, cl, cr, kd, fd, pp, bb, load_sem, send_sem, recv_sem):
     Z, R, NYW = tin_h.shape
     ZF, CX, CY = floor_h.shape
@@ -48,12 +48,8 @@
             [local_copy(mat_h.at[part, :, pl.ds(j * L, L)], mat.at[part, j, pl.ds(S, CX), :]) for j in range(NJ)]
             + [local_copy(floor_h.at[part, :, pl.ds(j * L, L)], floor0.at[part, j, pl.ds(S, CX), :])
                for j in range(NJ)])
-    get_tin = []
-    for q in range(NQ):
-        part = pl.ds(q * ZQ, ZQ)
-        get_tin.append(
-            [local_copy(tin_h.at[part, :, pl.ds(k * L, L)], tin0.at[pl.ds(q * ZQ + 1, ZQ), k, pl.ds(S, R), :])
-             for k in range(NK)] + [local_copy(flow_h.at[part], flow.at[part])])
+    get_tin = [local_copy(tin_h.at[:, :, pl.ds(k * L, L)], tin0.at[pl.ds(1, Z), k, pl.ds(S, R), :])
+               for k in range(NK)] + [local_copy(flow_h, flow)]
     get_cond.start()
     get_speeds.start()
 
@@ -73,7 +69,7 @@
         def _():
             hello(target)
 
-    for group in get_floor + get_tin:
+    for group in get_floor:
         for ld in group:
             ld.start()
 
@@ -112,40 +108,51 @@
         rup_ok, rdn_ok)
     c0 = both_ways([remote(cs.at[0:2], cl.at[0:2], me + 1)], [remote(cs.at[0:2], cr.at[0:2], me - 1)],
                    cup_ok, cdn_ok)
-    t1 = both_ways([remote(tin1.at[planes, :, S + R - 1, :], tin1.at[planes, :, lo, :], me + 1)],
-                   [remote(tin1.at[planes, :, S, :], tin1.at[planes, :, hi, :], me - 1)],
-                   up_ok, dn_ok)
     r1 = both_ways([remote(floor1.at[layers, :, S + CX - 1, :], floor1.at[layers, :, flo, :], me + ty)],
                    [remote(floor1.at[layers, :, S, :], floor1.at[layers, :, fhi, :], me - ty)],
                    rup_ok, rdn_ok)
     c1 = both_ways([remote(cs.at[2], cl.at[2], me + 1)], [remote(cs.at[2], cr.at[2], me - 1)],
                    cup_ok, cdn_ok)
 
-    def floor_part(field, t):
-        return field.at[0, :, pl.ds(pl.multiple_of(S + t * R, S), R), :]
-
-    def tin_part(field, t):
-        return field.at[1, pl.ds(NJ * t, NJ), pl.ds(S, R), :]
-
     def p_into(e):
         return pp.at[e, pl.ds(NJ * c, NJ), :, :]
 
     def b_into(e):
         return bb.at[e, :, pl.ds(pl.multiple_of(c * R, S), R), :]
 
-    def to_group(part, into):
-        out = []
-        for d in range(1, ty):
-            t = lax.rem(c + d, ty)
-            out.append(remote(part(t), into, base + t))
-        return out
-
-    p0 = to_group(functools.partial(floor_part, floor0), p_into(0))
-    b0 = to_group(functools.partial(tin_part, tin0), b_into(0))
-    p1 = to_group(functools.partial(floor_part, floor1), p_into(1))
-    b1 = to_group(functools.partial(tin_part, tin1), b_into(1))
-    own_p0, own_p1 = local_copy(floor_part(floor0, c), p_into(0)), local_copy(floor_part(floor1, c), p_into(1))
-    own_b0, own_b1 = local_copy(tin_part(tin0, c), b_into(0)), local_copy(tin_part(tin1, c), b_into(1))
+    def p_part(t):
+        return floor1.at[0, :, pl.ds(pl.multiple_of(S + t * R, S), R), :]
+
+    def b_part(t):
+        return tin1.at[1, pl.ds(NJ * t, NJ), pl.ds(S, R), :]
+
+    def p_parts(t):
+        return [(floor_h.at[0, pl.ds(pl.multiple_of(t * R, S), R), pl.ds(j * L, L)], pp.at[0, NJ * c + j])
+                for j in range(NJ)]
+
+    def b_parts(t):
+        return [(tin_h.at[0, :, pl.ds(pl.multiple_of((NJ * t + j) * L, L), L)],
+                 bb.at[0, j, pl.ds(pl.multiple_of(c * R, S), R), :]) for j in range(NJ)]
+
+    group = [lax.rem(c + d, ty) for d in range(1, ty)]
+    p0 = [remote(*m, base + t) for t in group for m in p_parts(t)]
+    b0 = [remote(*m, base + t) for t in group for m in b_parts(t)]
+    p1 = [remote(p_part(t), p_into(1), base + t) for t in group]
+    b1 = [remote(b_part(t), b_into(1), base + t) for t in group]
+    own0 = [local_copy(*m) for m in p_parts(c) + b_parts(c)]
+    own_p1, own_b1 = local_copy(p_part(c), p_into(1)), local_copy(b_part(c), b_into(1))
+    t1_first = next(links)
+
+    def t1(q):
+        part = pl.ds(q * ZQ + 1, ZQ)
+
+        def one(way, src, dst, target):
+            e = t1_first + 2 * q + way
+            return pltpu.make_async_remote_copy(
+                src_ref=tin1.at[part, :, src, :], dst_ref=tin1.at[part, :, dst, :], send_sem=send_sem.at[e],
+                recv_sem=recv_sem.at[e], device_id={"len": target}, device_id_type=pl.DeviceIdType.MESH)
+
+        return both_ways([one(0, S + R - 1, lo, me + 1)], [one(1, S, hi, me - 1)], up_ok, dn_ok)
 
     def start_if(msgs):
         for ok, _, copies in msgs:
@@ -167,6 +174,9 @@
             def _():
                 for m in copies:
                     m.wait_send()
+
+    for m in own0:
+        m.start()
 
     def clear(ok, fields, first):
         @pl.when(jnp.logical_not(ok))
@@ -198,7 +208,8 @@
         peers = peers + ok.astype(jnp.int32)
     pl.semaphore_wait(barrier, peers)
     start_if(r0)
-    start_if(t0)
+    for m in b0 + p0:
+        m.start()
 
     get_cond.wait()
     k0, k1, k2 = cond[0] * 0.5, cond[1] * 0.5, cond[2] * 0.5
@@ -208,7 +219,7 @@
 
     def pack_columns(slot, z, i, first, last):
         mine = lax.shift_right_logical(lane, 1) == z
-        both = pltpu.roll(jnp.where(lane_last, last, first), 2 * z + 1, 1)
+        both = pltpu.roll(jnp.where(lane_last, last, first), lax.rem(2 * z + 1 + L, L), 1)
         pltpu.store(cs.at[slot, pl.ds(i * S, S), :], both, mask=mine)
 
     def prepare(z, carry):
@@ -221,14 +232,29 @@
             pack_columns(1, z, i, floor0[z, 0, at, :], floor0[z, NJ - 1, at, :])
         return carry
 
+    def faces_y(z, carry):
+        for i in range(NI):
+            own = pl.ds(i * S, S)
+            k = [kh[z, j, pl.ds(S + i * S, S), :] for j in range(NJ)]
+            after = [pltpu.roll(v, L - 1, 1) for v in k]
+            before = [pltpu.roll(v, 1, 1) for v in k]
+            for j in range(NJ):
+                kyp[z, j, own, :] = k[j] + (
+                    after[j] if j == NJ - 1 else jnp.where(lane_last, after[j + 1], after[j]))
+                kym[z, j, own, :] = k[j] + (
+                    before[j] if j == 0 else jnp.where(lane_first, before[j - 1], before[j]))
+        return carry
+
     for q in range(FQ):
         for ld in get_floor[q]:
             ld.wait()
+        if q == FQ - 1:
+            for ld in get_tin:
+                ld.start()
         lax.fori_loop(q * ZC, (q + 1) * ZC, prepare, 0, unroll=PU)
     start_if(c0)
-    for m in p0:
-        m.start()
-    own_p0.start()
+    start_if(t0)
+    lax.fori_loop(0, ZF, faces_y, 0, unroll=PU)
 
     def tin_ghosts(e, src):
         for k in range(NK):
@@ -270,11 +296,12 @@
         tin_o[z, pl.ds(h * S, S), pl.ds(k * L, L)] = v
 
     def tin_range(src, put, first, last):
-        def body(z, carry):
-            tin_layer(src, put, z)
+        def body(step, carry):
+            for t in range(TU):
+                tin_layer(src, put, step * TU + t)
             return carry
 
-        lax.fori_loop(first, last, body, 0, unroll=TU)
+        lax.fori_loop(first, last, body, 0)
 
     def edge_flux(slot):
         for i in range(NI):
@@ -312,44 +339,36 @@
         for i in range(NI):
             own = pl.ds(i * S, S)
             g = [at(src, z, j, i) for j in range(NJ)]
-            if first:
-                k = [at(kh, z, j, i) for j in range(NJ)]
-                kr = [pltpu.roll(v, L - 1, 1) for v in k]
-                fy_k = []
-                for j in range(NJ):
-                    v = k[j] + (kr[j] if j == NJ - 1 else jnp.where(lane_last, kr[j + 1], kr[j]))
-                    ky[z, j, own, :] = v
-                    fy_k.append(v)
-            else:
-                fy_k = [ky[z, j, own, :] for j in range(NJ)]
             edge = pltpu.roll(fd[own, :], L - 1 - 2 * z, 1)
-            gr = [pltpu.roll(v, L - 1, 1) for v in g]
-            fy = []
+            after = [pltpu.roll(v, L - 1, 1) for v in g]
+            before = [pltpu.roll(v, 1, 1) for v in g]
             for j in range(NJ):
                 if j == NJ - 1:
-                    fy.append(jnp.where(lane_last, edge, fy_k[j] * (gr[j] - g[j])))
+                    fy = jnp.where(lane_last, edge, kyp[z, j, own, :] * (after[j] - g[j]))
                 else:
-                    fy.append(fy_k[j] * (jnp.where(lane_last, gr[j + 1], gr[j]) - g[j]))
-            fr = [pltpu.roll(v, 1, 1) for v in fy]
-            new = []
-            for j in range(NJ):
-                py = jnp.where(lane_first, fr[j - 1] if j else edge, fr[j])
+                    fy = kyp[z, j, own, :] * (jnp.where(lane_last, after[j + 1], after[j]) - g[j])
+                if j == 0:
+                    py = jnp.where(lane_first, edge, kym[z, j, own, :] * (g[j] - before[j]))
+                else:
+                    py = kym[z, j, own, :] * (g[j] - jnp.where(lane_first, before[j - 1], before[j]))
                 fx = flux_x(j, i)
                 rolled = pltpu.roll(fx, 1, 0)
                 px = jnp.where(row_first, rx[j], rolled)
                 rx[j] = rolled
                 if first:
-                    k_z = k[j] + at(kh, z + 1, j, i)
+                    k_z = at(kh, z, j, i) + at(kh, z + 1, j, i)
                     kz[z, j, own, :] = k_z
                 else:
                     k_z = kz[z, j, own, :]
                 fz = k_z * (at(src, z + 1, j, i) - g[j])
-                v = (g[j] + (fz - pz[j, own, :])) + ((fx - px) + (fy[j] - py))
+                put(z, j, i, (g[j] + (fz - pz[j, own, :])) + ((fx - px) + (fy - py)))
                 pz[j, own, :] = fz
-                put(z, j, i, v)
-                new.append(v)
-            if first:
-                pack_columns(2, z, i, new[0], new[NJ - 1])
+
+    def pack_new(z):
+        at = jnp.maximum(z, 0)
+        for i in range(NI):
+            own = pl.ds(S + i * S, S)
+            pack_columns(2, z, i, floor1[at, 0, own, :], floor1[at, NJ - 1, own, :])
 
     def put_floor1(z, j, i, v):
         floor1[z, j, pl.ds(S + i * S, S), :] = v
@@ -358,35 +377,18 @@
         floor_o[z, pl.ds(i * S, S), pl.ds(j * L, L)] = v
 
     def floor_sweep(first, src, put):
-        def body(z, carry):
-            floor_layer(first, src, put, z)
+        def body(step, carry):
+            if first:
+                for t in range(FU):
+                    pack_new((step - 1) * FU + t)
+            for t in range(FU):
+                floor_layer(first, src, put, step * FU + t)
             return carry
 
-        lax.fori_loop(0, ZF, body, 0, unroll=FU)
-
-    get_speeds.wait()
-    for ld in get_tin[0]:
-        ld.wait()
-    for m in b0:
-        m.start()
-    own_b0.start()
-    for m in p0:
-        m.wait_recv()
-    own_p0.wait()
-    tin_ghosts(0, tin0)
-    wait_recv_if(t0)
-    for q in range(NQ):
-        if q < NQ - 1:
-            for ld in get_tin[q + 1]:
-                ld.wait()
-        else:
-            tin_copy_last(tin0)
-        tin_range(tin0, put_tin1, q * ZQ, (q + 1) * ZQ)
-    tin_copy_last(tin1)
-    start_if(t1)
-    for m in b1:
-        m.start()
-    own_b1.start()
+        lax.fori_loop(0, ZF // FU, body, 0)
+        if first:
+            for t in range(FU):
+                pack_new(ZF - FU + t)
 
     wait_recv_if(r0)
 
@@ -397,25 +399,44 @@
         return carry
 
     lax.fori_loop(0, ZF, k_halo, 0, unroll=4)
+    for m in b0:
+        m.wait_recv()
+    for m in own0:
+        m.wait()
+    contact_flux(0, floor0)
     wait_recv_if(c0)
     edge_flux(1)
-    for m in b0:
-        m.wait_recv()
-    own_b0.wait()
-    contact_flux(0, floor0)
     floor_sweep(True, floor0, put_floor1)
     start_if(r1)
+    wait_send_if(c0)
     start_if(c1)
     for m in p1:
         m.start()
     own_p1.start()
 
-    wait_recv_if(t1)
-    for m in p1:
+    get_speeds.wait()
+    for ld in get_tin:
+        ld.wait()
+    for m in p0:
         m.wait_recv()
-    own_p1.wait()
-    tin_ghosts(1, tin1)
-    tin_range(tin1, put_tin_o, 0, Z)
+    tin_ghosts(0, tin0)
+    tin_copy_last(tin0)
+    wait_recv_if(t0)
+
+    def tin_part(q, carry):
+        tin_range(tin0, put_tin1, q * (ZQ // TU), (q + 1) * (ZQ // TU))
+        start_if(t1(q))
+
+        @pl.when(q == 0)
+        def _():
+            for m in b1:
+                m.start()
+            own_b1.start()
+
+        return carry
+
+    lax.fori_loop(0, NQ, tin_part, 0)
+    tin_copy_last(tin1)
 
     wait_recv_if(r1)
     wait_recv_if(c1)
@@ -426,7 +447,19 @@
     contact_flux(1, floor1)
     floor_sweep(False, floor1, put_floor_o)
 
-    for msgs in (t0, r0, c0, t1, r1, c1):
+    for m in p1:
+        m.wait_recv()
+    own_p1.wait()
+    tin_ghosts(1, tin1)
+
+    def tin_last(q, carry):
+        wait_recv_if(t1(q))
+        tin_range(tin1, put_tin_o, q * (ZQ // TU), (q + 1) * (ZQ // TU))
+        return carry
+
+    lax.fori_loop(0, NQ, tin_last, 0)
+
+    for msgs in [t0, r0, r1, c1] + [t1(q) for q in range(NQ)]:
         wait_send_if(msgs)
     for m in p0 + b0 + p1 + b1:
         m.wait_send()
@@ -441,8 +474,8 @@
     f32, i32 = jnp.float32, jnp.int32
     V = pltpu.VMEM
     tin_v, floor_v = V((Z + 2, NK, R + 2 * S, L), f32), V((ZF + 1, NJ, CX + 2 * S, L), f32)
-    n_local = 6 + FQ * 2 * NJ + NQ * (NK + 1)
-    n_remote = 2 * NK + 4 * NJ + 8 + 4 * (ty - 1)
+    n_local = 4 + FQ * 2 * NJ + NK + 1 + 2 * NJ
+    n_remote = 2 * NK + 4 * NJ + 6 + 2 * NQ + (2 * NJ + 2) * (ty - 1)
     tin_out, floor_out = pl.pallas_call(
         functools.partial(kernel, n, ty),
         out_shape=[V(tin_shape, f32), V(floor_shape, f32)],
@@ -451,7 +484,7 @@
         scratch_shapes=[
             pltpu.SMEM(speeds.shape, f32), pltpu.SMEM(conductivity.shape, f32),
             tin_v, V(tin_shape, i32), tin_v, floor_v, V((ZF, NJ, CX + 2 * S, L), i32), floor_v,
-            floor_v, V((ZF, NJ, CX + S, L), f32), V((ZF, NJ, CX, L), f32), V((ZF, NJ, CX, L), f32),
+            floor_v, V((ZF, NJ, CX + S, L), f32), V((ZF, NJ, CX, L), f32), V((ZF, NJ, CX, L), f32), V((ZF, NJ, CX, L), f32),
             V((NJ, CX, L), f32),
             V((3, CX, L), f32), V((3, CX, L), f32), V((3, CX, L), f32), V((CX, L), f32), V((CX, L), f32),
             V((2, NK, R, L), f32), V((2, NJ, CX, L), f32),

time: 51.9 us -> 30.4 us (0.59)
  the two profiles are of different devices: /device:TPU:1 before, /device:TPU:13 now
where the time goes in v2:
time: 30.4 us; the launch traced here: 30.2 us
  Pallas kernels  25.9 us (85%)
  local copies, waits for them, and re-layouts  3.68 us (12%)
  between operations  0.64 us (2%)
    pallas_call x1, Pallas kernels, local(): pl.pallas_call(functools.partial(kernel, n, ty), out_shape=[V(tin_shape,...  25.9 us
    unnamed x2, local copies, waits for them, and re-layouts  3.68 us

profile of v2, /device:TPU:13, one launch (start us, length us, event | category | flops | bytes accessed | tf_op | source)
XLA Modules:
  0.0 30.2 jit_solution(5772582111849202743)
XLA Ops:
  0.6 25.9 %shard_map.77 = (f32[64,16,1024]{2,1,0:T(8,128)S(1)}, f32[48,64,256]{2,1,0:T(8,128)S(1)}) custom-call(f32[64,16,1024]{2,1,0:T(8,128)} %tin_h.1, s32[64,16,1024]{2,1,0:T(8,128)} %flow_h.1, f32[2,64]{1,0:T(2,128)} %speeds_h.1, f32[48,64,256]{2,1,0:T(8,128)} %bitcast.4, s32[48,64,256]{2,1,0:T(8,128)} %bitcast.5, f32[3]{0:T(128)} %cond_h.1), custom_call_target="tpu_custom_call" | custom-call | flops 120000000 | bytes 23000000 | tf_op jit(solution)/shard_map/pallas_call | solution.py:479
  26.5 2.0 %copy.10 = f32[64,16,1024]{2,1,0:T(8,128)} copy(f32[64,16,1024]{2,1,0:T(8,128)S(1)} %get-tuple-element.6) | data formatting | bytes 8388608
  28.6 1.7 %copy.11 = f32[1,48,64,256]{3,2,1,0:T(8,128)} copy(f32[1,48,64,256]{3,2,1,0:T(8,128)S(1)} %bitcast.3) | data formatting | bytes 6291456

commit v3 on v2

--- a/solution.py
+++ b/solution.py
@@ -12,17 +12,69 @@
 HR = 0.2
 L = 128
 S = 8
-NQ = 4
+NQ = 2
 FQ = 2
 TU = 8
 FU = 8
 PU = 8
+VA = 38
+VB = 6
+
+
+def floor_layer(kh, src, put, z, kx, kyp, kym, kz, pz, fd):
+    NJ, NI = kyp.shape[1], kyp.shape[2] // S
+    first = kh is not None
+    lane = lax.broadcasted_iota(jnp.int32, (S, L), 1)
+    lane_first, lane_last = lane == 0, lane == L - 1
+    row_first = lax.broadcasted_iota(jnp.int32, (S, L), 0) == 0
+
+    def at(ref, p, j, i, shift=0):
+        return ref[p, j, pl.ds(S + i * S + shift, S), :]
+
+    def face_x(j, i):
+        if first:
+            v = at(kh, z, j, i) + at(kh, z, j, i, 1)
+            kx[z, j, pl.ds(S + i * S, S), :] = v
+            return v
+        return at(kx, z, j, i)
+
+    def flux_x(j, i):
+        return face_x(j, i) * (at(src, z, j, i, 1) - at(src, z, j, i))
+
+    rx = [pltpu.roll(flux_x(j, -1), 1, 0) for j in range(NJ)]
+    for i in range(NI):
+        own = pl.ds(i * S, S)
+        g = [at(src, z, j, i) for j in range(NJ)]
+        edge = pltpu.roll(fd[own, :], L - 1 - 2 * z, 1)
+        after = [pltpu.roll(v, L - 1, 1) for v in g]
+        before = [pltpu.roll(v, 1, 1) for v in g]
+        for j in range(NJ):
+            if j == NJ - 1:
+                fy = jnp.where(lane_last, edge, kyp[z, j, own, :] * (after[j] - g[j]))
+            else:
+                fy = kyp[z, j, own, :] * (jnp.where(lane_last, after[j + 1], after[j]) - g[j])
+            if j == 0:
+                py = jnp.where(lane_first, edge, kym[z, j, own, :] * (g[j] - before[j]))
+            else:
+                py = kym[z, j, own, :] * (g[j] - jnp.where(lane_first, before[j - 1], before[j]))
+            fx = flux_x(j, i)
+            rolled = pltpu.roll(fx, 1, 0)
+            px = jnp.where(row_first, rx[j], rolled)
+            rx[j] = rolled
+            if first:
+                k_z = at(kh, z, j, i) + at(kh, z + 1, j, i)
+                kz[z, j, own, :] = k_z
+            else:
+                k_z = kz[z, j, own, :]
+            fz = k_z * (at(src, z + 1, j, i) - g[j])
+            put(z, j, i, (g[j] + (fz - pz[j, own, :])) + ((fx - px) + (fy - py)))
+            pz[j, own, :] = fz
 
 
 def kernel(n, ty, tin_h, flow_h, speeds_h, floor_h, mat_h, cond_h,
-           tin_o, floor_o,
-           speeds, cond, tin0, flow, tin1, floor0, mat, floor1, kh, kx, kyp, kym, kz, pz,
-           cs, cl, cr, kd, fd, pp, bb, load_sem, send_sem, recv_sem):
+           tin_o, floor1, kx, kyp, kym, kz, pz, fd,
+           speeds, cond, tin0, flow, tin1, floor0, mat, kh,
+           cs, cl, cr, kd, pp, bb, load_sem, send_sem, recv_sem):
     Z, R, NYW = tin_h.shape
     ZF, CX, CY = floor_h.shape
     NH, NK = R // S, NYW // L
@@ -94,11 +146,6 @@
 
     lo, hi = S - 1, S + R
     flo, fhi = S - 1, S + CX
-    planes = pl.ds(1, Z)
-    t0 = both_ways(
-        [remote(tin_h.at[:, R - 1, pl.ds(k * L, L)], tin0.at[planes, k, lo, :], me + 1) for k in range(NK)],
-        [remote(tin_h.at[:, 0, pl.ds(k * L, L)], tin0.at[planes, k, hi, :], me - 1) for k in range(NK)],
-        up_ok, dn_ok)
     layers = pl.ds(0, ZF)
     r0 = both_ways(
         [remote(a.at[:, CX - 1, pl.ds(j * L, L)], b.at[layers, j, flo, :], me + ty)
@@ -141,18 +188,34 @@
     b1 = [remote(b_part(t), b_into(1), base + t) for t in group]
     own0 = [local_copy(*m) for m in p_parts(c) + b_parts(c)]
     own_p1, own_b1 = local_copy(p_part(c), p_into(1)), local_copy(b_part(c), b_into(1))
-    t1_first = next(links)
+    t0_first, t1_first = next(links), next(links) + 2 * NQ - 1
+
+    def tin_link(e, src, dst, target):
+        return pltpu.make_async_remote_copy(
+            src_ref=src, dst_ref=dst, send_sem=send_sem.at[e], recv_sem=recv_sem.at[e],
+            device_id={"len": target}, device_id_type=pl.DeviceIdType.MESH)
+
+    def t0_send(q):
+        part, into = pl.ds(q * ZQ, ZQ), pl.ds(q * ZQ + 1, ZQ)
+        e = t0_first + 2 * q
+        for ok, way, src, dst, target in ((up_ok, 0, R - 1, lo, me + 1), (dn_ok, 1, 0, hi, me - 1)):
+            @pl.when(ok)
+            def _():
+                for k in range(NK):
+                    tin_link(e + way, tin_h.at[part, src, pl.ds(k * L, L)], tin0.at[into, k, dst, :], target).start()
+
+    def t0(q):
+        part = pl.ds(q * ZQ + 1, ZQ)
+        e = t0_first + 2 * q
+        return both_ways([tin_link(e, tin0.at[part, :, lo, :], tin0.at[part, :, lo, :], me + 1)],
+                         [tin_link(e + 1, tin0.at[part, :, hi, :], tin0.at[part, :, hi, :], me - 1)], up_ok, dn_ok)
 
     def t1(q):
         part = pl.ds(q * ZQ + 1, ZQ)
-
-        def one(way, src, dst, target):
-            e = t1_first + 2 * q + way
-            return pltpu.make_async_remote_copy(
-                src_ref=tin1.at[part, :, src, :], dst_ref=tin1.at[part, :, dst, :], send_sem=send_sem.at[e],
-                recv_sem=recv_sem.at[e], device_id={"len": target}, device_id_type=pl.DeviceIdType.MESH)
-
-        return both_ways([one(0, S + R - 1, lo, me + 1)], [one(1, S, hi, me - 1)], up_ok, dn_ok)
+        e = t1_first + 2 * q
+        return both_ways(
+            [tin_link(e, tin1.at[part, :, S + R - 1, :], tin1.at[part, :, lo, :], me + 1)],
+            [tin_link(e + 1, tin1.at[part, :, S, :], tin1.at[part, :, hi, :], me - 1)], up_ok, dn_ok)
 
     def start_if(msgs):
         for ok, _, copies in msgs:
@@ -210,6 +273,8 @@
     start_if(r0)
     for m in b0 + p0:
         m.start()
+    for q in range(NQ):
+        t0_send(q)
 
     get_cond.wait()
     k0, k1, k2 = cond[0] * 0.5, cond[1] * 0.5, cond[2] * 0.5
@@ -253,7 +318,6 @@
                 ld.start()
         lax.fori_loop(q * ZC, (q + 1) * ZC, prepare, 0, unroll=PU)
     start_if(c0)
-    start_if(t0)
     lax.fori_loop(0, ZF, faces_y, 0, unroll=PU)
 
     def tin_ghosts(e, src):
@@ -321,49 +385,6 @@
                 at = pl.ds(i * S, S)
                 pz[j, at, :] = HR * (src[0, j, pl.ds(S + i * S, S), :] - bb[e, j, at, :])
 
-    def floor_layer(first, src, put, z):
-        def at(ref, p, j, i, shift=0):
-            return ref[p, j, pl.ds(S + i * S + shift, S), :]
-
-        def face_x(j, i):
-            if first:
-                v = at(kh, z, j, i) + at(kh, z, j, i, 1)
-                kx[z, j, pl.ds(S + i * S, S), :] = v
-                return v
-            return at(kx, z, j, i)
-
-        def flux_x(j, i):
-            return face_x(j, i) * (at(src, z, j, i, 1) - at(src, z, j, i))
-
-        rx = [pltpu.roll(flux_x(j, -1), 1, 0) for j in range(NJ)]
-        for i in range(NI):
-            own = pl.ds(i * S, S)
-            g = [at(src, z, j, i) for j in range(NJ)]
-            edge = pltpu.roll(fd[own, :], L - 1 - 2 * z, 1)
-            after = [pltpu.roll(v, L - 1, 1) for v in g]
-            before = [pltpu.roll(v, 1, 1) for v in g]
-            for j in range(NJ):
-                if j == NJ - 1:
-                    fy = jnp.where(lane_last, edge, kyp[z, j, own, :] * (after[j] - g[j]))
-                else:
-                    fy = kyp[z, j, own, :] * (jnp.where(lane_last, after[j + 1], after[j]) - g[j])
-                if j == 0:
-                    py = jnp.where(lane_first, edge, kym[z, j, own, :] * (g[j] - before[j]))
-                else:
-                    py = kym[z, j, own, :] * (g[j] - jnp.where(lane_first, before[j - 1], before[j]))
-                fx = flux_x(j, i)
-                rolled = pltpu.roll(fx, 1, 0)
-                px = jnp.where(row_first, rx[j], rolled)
-                rx[j] = rolled
-                if first:
-                    k_z = at(kh, z, j, i) + at(kh, z + 1, j, i)
-                    kz[z, j, own, :] = k_z
-                else:
-                    k_z = kz[z, j, own, :]
-                fz = k_z * (at(src, z + 1, j, i) - g[j])
-                put(z, j, i, (g[j] + (fz - pz[j, own, :])) + ((fx - px) + (fy - py)))
-                pz[j, own, :] = fz
-
     def pack_new(z):
         at = jnp.maximum(z, 0)
         for i in range(NI):
@@ -373,57 +394,23 @@
     def put_floor1(z, j, i, v):
         floor1[z, j, pl.ds(S + i * S, S), :] = v
 
-    def put_floor_o(z, j, i, v):
-        floor_o[z, pl.ds(i * S, S), pl.ds(j * L, L)] = v
-
-    def floor_sweep(first, src, put):
-        def body(step, carry):
-            if first:
-                for t in range(FU):
-                    pack_new((step - 1) * FU + t)
-            for t in range(FU):
-                floor_layer(first, src, put, step * FU + t)
-            return carry
-
-        lax.fori_loop(0, ZF // FU, body, 0)
-        if first:
-            for t in range(FU):
-                pack_new(ZF - FU + t)
-
-    wait_recv_if(r0)
-
-    def k_halo(z, carry):
-        for j in range(NJ):
-            for ok, at in ((rdn_ok, pl.ds(0, S)), (rup_ok, pl.ds(S + CX, S))):
-                kh[z, j, at, :] = lookup(mat[z, j, at, :]) * ok.astype(jnp.float32)
-        return carry
-
-    lax.fori_loop(0, ZF, k_halo, 0, unroll=4)
-    for m in b0:
-        m.wait_recv()
-    for m in own0:
-        m.wait()
-    contact_flux(0, floor0)
-    wait_recv_if(c0)
-    edge_flux(1)
-    floor_sweep(True, floor0, put_floor1)
-    start_if(r1)
-    wait_send_if(c0)
-    start_if(c1)
-    for m in p1:
-        m.start()
-    own_p1.start()
+    def floor_step(step, carry):
+        for t in range(FU):
+            pack_new((step - 1) * FU + t)
+        for t in range(FU):
+            floor_layer(kh, floor0, put_floor1, step * FU + t, kx, kyp, kym, kz, pz, fd)
+        return carry
 
     get_speeds.wait()
-    for ld in get_tin:
+    for ld in get_tin + own0:
         ld.wait()
     for m in p0:
         m.wait_recv()
     tin_ghosts(0, tin0)
     tin_copy_last(tin0)
-    wait_recv_if(t0)
-
-    def tin_part(q, carry):
+
+    def tin_first_part(q, carry):
+        wait_recv_if(t0(q))
         tin_range(tin0, put_tin1, q * (ZQ // TU), (q + 1) * (ZQ // TU))
         start_if(t1(q))
 
@@ -435,34 +422,92 @@
 
         return carry
 
-    lax.fori_loop(0, NQ, tin_part, 0)
+    lax.fori_loop(0, NQ, tin_first_part, 0)
     tin_copy_last(tin1)
 
-    wait_recv_if(r1)
-    wait_recv_if(c1)
+    wait_recv_if(r0)
+
+    def k_halo(z, carry):
+        for j in range(NJ):
+            for ok, at in ((rdn_ok, pl.ds(0, S)), (rup_ok, pl.ds(S + CX, S))):
+                kh[z, j, at, :] = lookup(mat[z, j, at, :]) * ok.astype(jnp.float32)
+        return carry
+
+    lax.fori_loop(0, ZF, k_halo, 0, unroll=4)
+    for m in b0:
+        m.wait_recv()
+    contact_flux(0, floor0)
+    wait_recv_if(c0)
+    edge_flux(1)
+    lax.fori_loop(0, ZF // FU, floor_step, 0)
+    for m in p1:
+        m.start()
+    own_p1.start()
+    for t in range(FU):
+        pack_new(ZF - FU + t)
+    start_if(c1)
+    start_if(r1)
+
+    def tin_last(step, carry):
+        q = lax.rem(step + 1, NQ)
+
+        @pl.when(step == 0)
+        def _():
+            wait_recv_if(t1(0))
+
+        @pl.when(step < NQ - 1)
+        def _():
+            wait_recv_if(t1(q))
+
+        @pl.when(step == NQ - 1)
+        def _():
+            for m in p1:
+                m.wait_recv()
+            own_p1.wait()
+            tin_ghosts(1, tin1)
+
+        tin_range(tin1, put_tin_o, q * (ZQ // TU), (q + 1) * (ZQ // TU))
+        return carry
+
+    lax.fori_loop(0, NQ, tin_last, 0)
+
     for m in b1:
         m.wait_recv()
     own_b1.wait()
+    contact_flux(1, floor1)
+    wait_recv_if(c1)
     edge_flux(2)
-    contact_flux(1, floor1)
-    floor_sweep(False, floor1, put_floor_o)
-
-    for m in p1:
-        m.wait_recv()
-    own_p1.wait()
-    tin_ghosts(1, tin1)
-
-    def tin_last(q, carry):
-        wait_recv_if(t1(q))
-        tin_range(tin1, put_tin_o, q * (ZQ // TU), (q + 1) * (ZQ // TU))
-        return carry
-
-    lax.fori_loop(0, NQ, tin_last, 0)
-
-    for msgs in [t0, r0, r1, c1] + [t1(q) for q in range(NQ)]:
+    wait_recv_if(r1)
+
+    for msgs in [c0, r0, r1, c1] + [t(q) for t in (t0, t1) for q in range(NQ)]:
         wait_send_if(msgs)
     for m in p0 + b0 + p1 + b1:
         m.wait_send()
+
+
+def finish(tin_v, floor1, kx, kyp, kym, kz, pz_in, fd, tin_o, floor_o, floor_v, pz, sems):
+    ZF, NJ, CX = kyp.shape[:3]
+    out = pltpu.make_async_copy(tin_v, tin_o, sems.at[0])
+    out.start()
+    pz[...] = pz_in[...]
+
+    def put(z, j, i, v):
+        floor_v[z, pl.ds(i * S, S), pl.ds(j * L, L)] = v
+
+    def part(step):
+        rows = pl.ds(step * FU, FU)
+        return pltpu.make_async_copy(floor_v.at[rows], floor_o.at[rows], sems.at[1 + step])
+
+    def body(step, carry):
+        for t in range(FU):
+            floor_layer(None, floor1, put, step * FU + t, kx, kyp, kym, kz, pz, fd)
+        part(step).start()
+        return carry
+
+    lax.fori_loop(0, ZF // FU, body, 0)
+    for step in range(ZF // FU):
+        part(step).wait()
+    out.wait()
 
 
 def local(n, ty, tin_temp, flow_code, speeds, floor_temp, material, conductivity):
@@ -475,28 +520,37 @@
     V = pltpu.VMEM
     tin_v, floor_v = V((Z + 2, NK, R + 2 * S, L), f32), V((ZF + 1, NJ, CX + 2 * S, L), f32)
     n_local = 4 + FQ * 2 * NJ + NK + 1 + 2 * NJ
-    n_remote = 2 * NK + 4 * NJ + 6 + 2 * NQ + (2 * NJ + 2) * (ty - 1)
-    tin_out, floor_out = pl.pallas_call(
+    n_remote = 4 * NJ + 6 + 4 * NQ + (2 * NJ + 2) * (ty - 1)
+    face = V((ZF, NJ, CX, L), f32)
+    middle = pl.pallas_call(
         functools.partial(kernel, n, ty),
-        out_shape=[V(tin_shape, f32), V(floor_shape, f32)],
+        out_shape=[V(tin_shape, f32), floor_v, V((ZF, NJ, CX + S, L), f32), face, face, face,
+                   V((NJ, CX, L), f32), V((CX, L), f32)],
         in_specs=[pl.BlockSpec(memory_space=pltpu.HBM)] * 6,
-        out_specs=[pl.BlockSpec(memory_space=pltpu.VMEM)] * 2,
+        out_specs=[pl.BlockSpec(memory_space=pltpu.VMEM)] * 8,
         scratch_shapes=[
             pltpu.SMEM(speeds.shape, f32), pltpu.SMEM(conductivity.shape, f32),
             tin_v, V(tin_shape, i32), tin_v, floor_v, V((ZF, NJ, CX + 2 * S, L), i32), floor_v,
-            floor_v, V((ZF, NJ, CX + S, L), f32), V((ZF, NJ, CX, L), f32), V((ZF, NJ, CX, L), f32), V((ZF, NJ, CX, L), f32),
-            V((NJ, CX, L), f32),
-            V((3, CX, L), f32), V((3, CX, L), f32), V((3, CX, L), f32), V((CX, L), f32), V((CX, L), f32),
+            V((3, CX, L), f32), V((3, CX, L), f32), V((3, CX, L), f32), V((CX, L), f32),
             V((2, NK, R, L), f32), V((2, NJ, CX, L), f32),
             pltpu.SemaphoreType.DMA((n_local,)),
             pltpu.SemaphoreType.DMA((n_remote,)),
             pltpu.SemaphoreType.DMA((n_remote,)),
         ],
         compiler_params=pltpu.CompilerParams(
-            collective_id=0, has_side_effects=True, vmem_limit_bytes=52 * 1024 * 1024),
+            collective_id=0, has_side_effects=True, vmem_limit_bytes=VA * 1024 * 1024),
         cost_estimate=pl.CostEstimate(flops=120_000_000, bytes_accessed=23_000_000, transcendentals=0),
     )(tin_temp, flow_code, pltpu.with_memory_space_constraint(speeds, pltpu.HBM), floor_temp[0],
       material[0], pltpu.with_memory_space_constraint(conductivity, pltpu.HBM))
+    tin_out, floor_out = pl.pallas_call(
+        finish,
+        out_shape=[jax.ShapeDtypeStruct(tin_shape, f32), jax.ShapeDtypeStruct(floor_shape, f32)],
+        in_specs=[pl.BlockSpec(memory_space=pltpu.VMEM)] * 8,
+        out_specs=[pl.BlockSpec(memory_space=pltpu.HBM)] * 2,
+        scratch_shapes=[V(floor_shape, f32), V((NJ, CX, L), f32), pltpu.SemaphoreType.DMA((1 + ZF // FU,))],
+        compiler_params=pltpu.CompilerParams(vmem_limit_bytes=VB * 1024 * 1024),
+        cost_estimate=pl.CostEstimate(flops=20_000_000, bytes_accessed=8_000_000, transcendentals=0),
+    )(*middle)
     return tin_out, floor_out[None]
 
 

time: 30.4 us -> 28.2 us (0.928)
  the two profiles are of different devices: /device:TPU:13 before, /device:TPU:1 now
where the time goes in v3:
time: 28.2 us; the launch traced here: 28 us
  Pallas kernels  27.4 us (97%)
  between operations  0.64 us (2%)
    pallas_call x1, Pallas kernels, local(): pl.pallas_call(functools.partial(kernel, n, ty), out_shape=[V(tin_shape,...  24 us
    pallas_call x1, Pallas kernels, local(): pl.pallas_call(finish, out_shape=[jax.ShapeDtypeStruct(tin_shape, f32), j...  3.42 us

profile of v3, /device:TPU:1, one launch (start us, length us, event | category | flops | bytes accessed | tf_op | source)
XLA Modules:
  0.0 28.0 jit_solution(500662537952780636)
XLA Ops:
  0.6 24.0 %shard_map.77 = (f32[64,16,1024]{2,1,0:T(8,128)S(1)}, f32[49,2,80,128]{3,2,1,0:T(8,128)S(1)}, f32[48,2,72,128]{3,2,1,0:T(8,128)S(1)}, f32[48,2,64,128]{3,2,1,0:T...) custom-call(f32[64,16,1024]{2,1,0:T(8,128)} %tin_h.1, ...), custom_call_target="tpu_custom_call" | custom-call | flops 120000000 | bytes 23000000 | tf_op jit(solution)/shard_map/pallas_call | solution.py:525
  24.6 3.4 %shard_map.78 = (f32[64,16,1024]{2,1,0:T(8,128)}, f32[48,64,256]{2,1,0:T(8,128)}) custom-call(f32[64,16,1024]{2,1,0:T(8,128)S(1)} %get-tuple-element.12.tin_v, f32[49,2,80,128]{3,2,1,0:T(8,128)S(1)} %get-tuple-element.13.floor1, f32[48,2,72,128]{3,2,1,0:T(8,128)S(1)} %get-tuple-element.14.kx, f32[48,2,64,128]{3,2,1,0:T(8,128)S(1)} %get-tuple-element.15.kyp, ...), custom_call_target="tpu_custom_call" | custom-call | flops 20000000 | bytes 8000000 | tf_op jit(solution)/shard_map/pallas_call | solution.py:545

commit v4 on v3

--- a/solution.py
+++ b/solution.py
@@ -16,7 +16,7 @@
 FQ = 2
 TU = 8
 FU = 8
-PU = 8
+PU = 4
 VA = 38
 VB = 6
 
@@ -195,10 +195,12 @@
             src_ref=src, dst_ref=dst, send_sem=send_sem.at[e], recv_sem=recv_sem.at[e],
             device_id={"len": target}, device_id_type=pl.DeviceIdType.MESH)
 
-    def t0_send(q):
+    cross_up, cross_dn = jnp.logical_and(up_ok, c == ty - 1), jnp.logical_and(dn_ok, c == 0)
+
+    def t0_send(q, oks):
         part, into = pl.ds(q * ZQ, ZQ), pl.ds(q * ZQ + 1, ZQ)
         e = t0_first + 2 * q
-        for ok, way, src, dst, target in ((up_ok, 0, R - 1, lo, me + 1), (dn_ok, 1, 0, hi, me - 1)):
+        for ok, way, src, dst, target in ((oks[0], 0, R - 1, lo, me + 1), (oks[1], 1, 0, hi, me - 1)):
             @pl.when(ok)
             def _():
                 for k in range(NK):
@@ -273,8 +275,9 @@
     start_if(r0)
     for m in b0 + p0:
         m.start()
-    for q in range(NQ):
-        t0_send(q)
+    t0_send(0, (up_ok, dn_ok))
+    for q in range(1, NQ):
+        t0_send(q, (cross_up, cross_dn))
 
     get_cond.wait()
     k0, k1, k2 = cond[0] * 0.5, cond[1] * 0.5, cond[2] * 0.5
@@ -318,6 +321,8 @@
                 ld.start()
         lax.fori_loop(q * ZC, (q + 1) * ZC, prepare, 0, unroll=PU)
     start_if(c0)
+    for q in range(1, NQ):
+        t0_send(q, (cup_ok, cdn_ok))
     lax.fori_loop(0, ZF, faces_y, 0, unroll=PU)
 
     def tin_ghosts(e, src):
@@ -409,7 +414,13 @@
     tin_ghosts(0, tin0)
     tin_copy_last(tin0)
 
-    def tin_first_part(q, carry):
+    def k_halo(z, carry):
+        for j in range(NJ):
+            for ok, at in ((rdn_ok, pl.ds(0, S)), (rup_ok, pl.ds(S + CX, S))):
+                kh[z, j, at, :] = lookup(mat[z, j, at, :]) * ok.astype(jnp.float32)
+        return carry
+
+    def first_sweep(q, carry):
         wait_recv_if(t0(q))
         tin_range(tin0, put_tin1, q * (ZQ // TU), (q + 1) * (ZQ // TU))
         start_if(t1(q))
@@ -419,53 +430,39 @@
             for m in b1:
                 m.start()
             own_b1.start()
-
-        return carry
-
-    lax.fori_loop(0, NQ, tin_first_part, 0)
+            wait_recv_if(r0)
+            lax.fori_loop(0, ZF, k_halo, 0, unroll=4)
+            for m in b0:
+                m.wait_recv()
+            contact_flux(0, floor0)
+            wait_recv_if(c0)
+            edge_flux(1)
+
+        steps = ZF // FU // NQ
+        lax.fori_loop(q * steps, (q + 1) * steps, floor_step, 0)
+
+        @pl.when(q == 0)
+        def _():
+            for m in p1:
+                m.start()
+            own_p1.start()
+
+        return carry
+
+    lax.fori_loop(0, NQ, first_sweep, 0)
     tin_copy_last(tin1)
-
-    wait_recv_if(r0)
-
-    def k_halo(z, carry):
-        for j in range(NJ):
-            for ok, at in ((rdn_ok, pl.ds(0, S)), (rup_ok, pl.ds(S + CX, S))):
-                kh[z, j, at, :] = lookup(mat[z, j, at, :]) * ok.astype(jnp.float32)
-        return carry
-
-    lax.fori_loop(0, ZF, k_halo, 0, unroll=4)
-    for m in b0:
-        m.wait_recv()
-    contact_flux(0, floor0)
-    wait_recv_if(c0)
-    edge_flux(1)
-    lax.fori_loop(0, ZF // FU, floor_step, 0)
-    for m in p1:
-        m.start()
-    own_p1.start()
     for t in range(FU):
         pack_new(ZF - FU + t)
     start_if(c1)
     start_if(r1)
 
-    def tin_last(step, carry):
-        q = lax.rem(step + 1, NQ)
-
-        @pl.when(step == 0)
-        def _():
-            wait_recv_if(t1(0))
-
-        @pl.when(step < NQ - 1)
-        def _():
-            wait_recv_if(t1(q))
-
-        @pl.when(step == NQ - 1)
-        def _():
-            for m in p1:
-                m.wait_recv()
-            own_p1.wait()
-            tin_ghosts(1, tin1)
-
+    for m in p1:
+        m.wait_recv()
+    own_p1.wait()
+    tin_ghosts(1, tin1)
+
+    def tin_last(q, carry):
+        wait_recv_if(t1(q))
         tin_range(tin1, put_tin_o, q * (ZQ // TU), (q + 1) * (ZQ // TU))
         return carry
 

time: 28.2 us -> 26.2 us (0.929)
  Pallas kernels: 27.4 us -> 25.3 us
    pallas_call x1, Pallas kernels: 24 us -> 21.9 us  [local(): pl.pallas_call(functools.partial(kernel, n, ty), out_shape=[V(tin_shape,...]
where the time goes in v4:
time: 26.2 us; the launch traced here: 25.9 us
  Pallas kernels  25.3 us (97%)
  between operations  0.64 us (2%)
    pallas_call x1, Pallas kernels, local(): pl.pallas_call(functools.partial(kernel, n, ty), out_shape=[V(tin_shape,...  21.9 us
    pallas_call x1, Pallas kernels, local(): pl.pallas_call(finish, out_shape=[jax.ShapeDtypeStruct(tin_shape, f32), j...  3.42 us

profile of v4, /device:TPU:1, one launch (start us, length us, event | category | flops | bytes accessed | tf_op | source)
XLA Modules:
  0.0 25.9 jit_solution(16997516418920819947)
XLA Ops:
  0.6 21.9 %shard_map.77 = (f32[64,16,1024]{2,1,0:T(8,128)S(1)}, f32[49,2,80,128]{3,2,1,0:T(8,128)S(1)}, f32[48,2,72,128]{3,2,1,0:T(8,128)S(1)}, f32[48,2,64,128]{3,2,1,0:T...) custom-call(f32[64,16,1024]{2,1,0:T(8,128)} %tin_h.1, ...), custom_call_target="tpu_custom_call" | custom-call | flops 120000000 | bytes 23000000 | tf_op jit(solution)/shard_map/pallas_call | solution.py:522
  22.5 3.4 %shard_map.78 = (f32[64,16,1024]{2,1,0:T(8,128)}, f32[48,64,256]{2,1,0:T(8,128)}) custom-call(f32[64,16,1024]{2,1,0:T(8,128)S(1)} %get-tuple-element.12.tin_v, f32[49,2,80,128]{3,2,1,0:T(8,128)S(1)} %get-tuple-element.13.floor1, f32[48,2,72,128]{3,2,1,0:T(8,128)S(1)} %get-tuple-element.14.kx, f32[48,2,64,128]{3,2,1,0:T(8,128)S(1)} %get-tuple-element.15.kyp, ...), custom_call_target="tpu_custom_call" | custom-call | flops 20000000 | bytes 8000000 | tf_op jit(solution)/shard_map/pallas_call | solution.py:542
